TPU v7x, 32 devices: a whole 2x2x4 slice. The times are simulated.
32 devices in a mesh: panel: 4 (over y, x), leaf: 8 (over z, core).
Axes of the slice: x: 2, y: 2, z: 4, core: 2. Of those that a mesh axis runs over, the one named last changes fastest.
Arguments:
- excitation: bfloat16 [2, 128, 98304], P(None, None, ('panel', 'leaf')), may hold values from -6 to 6
- point_order: int32 [32, 3072], P(('panel', 'leaf')), may hold values from 0 to 3071, each once within a row
- projection: bfloat16 [2, 256, 98304], P(None, None, ('panel', 'leaf')), may hold values from -0.078125 to 0.078125
- transfer: bfloat16 [3, 2, 8192, 512], P(None, None, ('panel', 'leaf')), may hold values from -0.1875 to 0.1875
- expansion: bfloat16 [2, 256, 98304], P(None, None, ('panel', 'leaf')), may hold values from -0.125 to 0.125
Outputs:
- response: bfloat16 [2, 128, 98304], P(None, None, ('panel', 'leaf'))
Inputs may be any that keep to these rules, and one draw needn't show every extreme that they name: Each row of point_order holds every number of 0 to 3071 once.
All inputs are finite; a program needn't handle non-finite values.
Results may differ from a plain program's by a relative error of at most 0.018.
Values may be sent and summed in bfloat16 or wider, within the bound.
A program may use at most 64 MiB of HBM per device.

v0:
```python
import jax
import jax.numpy as jnp
from jax import lax
from jax.sharding import PartitionSpec as P


def partner_2(block, axis, stride):
    count = lax.axis_size(axis)
    route = []
    for low in range(count):
        high = low | 1 << stride
        if high != low and high < count:
            route += [(low, high), (high, low)]
    return lax.ppermute(block, axis, route)


def complex_dot(first_matrix, second_matrix, first_dim, second_dim):
    contract = (((first_dim,), (second_dim,)), ((), ()))

    def real_dot(first_part, second_part):
        return lax.dot_general(
            first_part, second_part, contract, preferred_element_type=jnp.float32
        )

    real_part = real_dot(first_matrix[0], second_matrix[0]) - real_dot(
        first_matrix[1], second_matrix[1]
    )
    imag_part = real_dot(first_matrix[0], second_matrix[1]) + real_dot(
        first_matrix[1], second_matrix[0]
    )
    return jnp.stack((real_part, imag_part))


def per_device(excitation, point_order, projection, transfer, expansion):
    gathered = jnp.take(excitation, point_order[0], axis=2)
    coefficients = complex_dot(projection, gathered, 1, 1).astype(jnp.bfloat16)
    position = lax.axis_index("leaf")
    rank_width = coefficients.shape[1]
    for level in range(lax.axis_size("leaf").bit_length() - 1):
        partner = partner_2(coefficients, "leaf", level)
        upper_bit = position >> level & 1 == 1
        matrix = transfer[level]
        first_block = matrix[:, :, :rank_width]
        second_block = matrix[:, :, rank_width:]
        own_matrix = jnp.where(upper_bit, second_block, first_block)
        other_matrix = jnp.where(upper_bit, first_block, second_block)
        own_term = complex_dot(own_matrix, coefficients, 1, 0)
        partner_term = complex_dot(other_matrix, partner, 1, 0)
        coefficients = (own_term + partner_term).astype(jnp.bfloat16)
    summed = jnp.sum(
        lax.all_gather(coefficients[None], "panel", axis=0, tiled=True).astype(jnp.float32), axis=0
    )
    summed = summed.astype(jnp.bfloat16)
    result = complex_dot(summed, expansion, 0, 0)
    return result.astype(jnp.bfloat16)


def solution(mesh):
    in_specs = (
        P(None, None, ("panel", "leaf")),
        P(("panel", "leaf"), None),
        P(None, None, ("panel", "leaf")),
        P(None, None, ("panel", "leaf"), None),
        P(None, None, ("panel", "leaf")),
    )
    out_specs = P(None, None, ("panel", "leaf"))
    return jax.shard_map(
        per_device, mesh=mesh, in_specs=in_specs, out_specs=out_specs, check_vma=False
    )
```

profile of v0, /device:TPU:0, one launch (start us, length us, event | category | flops | bytes accessed | tf_op | source)
XLA Modules:
  0.0 72.1 jit_solution(16937209792244639220)
XLA Ops:
  0.0 3.6 %copy.10 = bf16[2,128,3072]{1,0,2:T(2,128)(2,1)S(1)} copy(bf16[2,128,3072]{2,1,0:T(8,128)(2,1)} %param.5) | data formatting | bytes 3145728 | tf_op args[0]
  3.7 10.4 %gather_fusion = bf16[3072,2,128]{2,1,0:T(2,128)(2,1)S(1)} fusion(bf16[2,128,3072]{1,0,2:T(2,128)(2,1)S(1)} %copy.10, s32[3072]{0:T(1024)S(1)} %broadcast_clamp_fusion), kind=kCustom, calls=%fused_computation | custom fusion | bytes 3158016 | tf_op jit(solution)/shard_map/jit(_take)/gather | solution.py:35
  14.1 11.1 %fusion.18 = bf16[2,128,3072]{1,0,2:T(2,128)(2,1)S(1)} fusion(bf16[3072,2,128]{2,1,0:T(2,128)(2,1)S(1)} %gather_fusion, pred[3072]{0:T(1024)(128)(4,1)S(1)} %compare_and_fusion), kind=kLoop, calls=%fused_computation.23 | loop fusion | flops 786432 | bytes 3148800 | tf_op jit(solution)/shard_map/jit(_take)/select_n | solution.py:35
  25.2 2.2 %fusion.70 = (bf16[1,128,3072]{1,0,2:T(2,128)(2,1)S(1)}, bf16[1,128,3072]{1,0,2:T(2,128)(2,1)S(1)}) fusion(bf16[2,128,3072]{1,0,2:T(2,128)(2,1)S(1)} %fusion.18), kind=kLoop, calls=%fused_computation.120 | loop fusion | bytes 3145728 | tf_op jit(solution)/shard_map/slice | solution.py:26
  27.5 2.9 %copy.12 = bf16[1,128,3072]{2,1,0:T(8,128)(2,1)} copy(bf16[1,128,3072]{1,0,2:T(2,128)(2,1)S(1)} %get-tuple-element.8) | data formatting | bytes 1572864 | tf_op jit(solution)/shard_map/slice | solution.py:26
  30.3 1.6 %copy.11 = bf16[1,128,3072]{2,1,0:T(8,128)(2,1)S(1)} copy(bf16[1,128,3072]{1,0,2:T(2,128)(2,1)S(1)} %get-tuple-element.9) | data formatting | bytes 1572864 | tf_op jit(solution)/shard_map/slice | solution.py:25
  32.0 2.2 %fusion.12 = f32[128,256]{1,0:T(8,128)S(1)} fusion(bf16[2,256,3072]{2,1,0:T(8,128)(2,1)} %param.7, bf16[1,128,3072]{2,1,0:T(8,128)(2,1)S(1)} %copy-done.2), kind=kOutput, calls=%fused_computation.17 | convolution fusion | flops 201326592 | bytes 2490368 | tf_op jit(solution)/shard_map/dot_general | solution.py:21
  34.2 2.1 %fusion.10 = f32[128,256]{1,0:T(8,128)S(1)} fusion(bf16[2,256,3072]{2,1,0:T(8,128)(2,1)} %param.7, bf16[1,128,3072]{2,1,0:T(8,128)(2,1)S(1)} %copy.11), kind=kOutput, calls=%fused_computation.15 | convolution fusion | flops 201326592 | bytes 2490368 | tf_op jit(solution)/shard_map/dot_general | solution.py:21
  36.3 0.7 fusion.48
  37.0 0.7 fusion.45
  37.7 0.5 collective-permute-start
  38.2 0.2 copy-done.1
  38.7 0.2 fusion.62
  39.0 0.2 fusion.44
  39.2 0.2 fusion.43
  39.6 0.2 fusion.64
  39.8 0.2 fusion.42
  40.0 0.2 fusion.41
  40.2 3.1 %collective-permute-start.1 = (bf16[2,256,128]{2,1,0:T(8,128)(2,1)S(1)}, bf16[2,256,128]{2,1,0:T(8,128)(2,1)S(1)}, u32[]{:S(2)}, u32[]{:S(2)}) collective-permute-start(bf16[2,256,128]{2,1,0:T(8,128)(2,1)S(1)} %fusion.55), channel_id=1, source_target_pairs={{0,2},{2,0},{1,3},{3,1},{4,6},{6,4},{5,7},{7,5},{8,10},{10,8},{9,1... | collective-permute-start | bytes 393224 | tf_op jit(solution)/shard_map/ppermute | solution.py:14
  43.8 0.2 fusion.39
  44.0 2.8 %collective-permute-done.1 = bf16[2,256,128]{2,1,0:T(8,128)(2,1)S(1)} collective-permute-done((bf16[2,256,128]{2,1,0:T(8,128)(2,1)S(1)}, bf16[2,256,128]{2,1,0:T(8,128)(2,1)S(1)}, u32[]{:S(2)}, u32[]{:S(2)}) %collective-permute-start.1) | collective-permute-done | bytes 131104 | tf_op jit(solution)/shard_map/ppermute | solution.py:14
  47.6 2.8 %collective-permute-start.2 = (bf16[2,256,128]{2,1,0:T(8,128)(2,1)S(1)}, bf16[2,256,128]{2,1,0:T(8,128)(2,1)S(1)}, u32[]{:S(2)}, u32[]{:S(2)}) collective-permute-start(bf16[2,256,128]{2,1,0:T(8,128)(2,1)S(1)} %fusion.56), channel_id=1, source_target_pairs={{0,4},{4,0},{1,5},{5,1},{2,6},{6,2},{3,7},{7,3},{8,12},{12,8},{9,1... | collective-permute-start | bytes 393224 | tf_op jit(solution)/shard_map/ppermute | solution.py:14
  50.9 0.2 fusion.35
  51.1 5.0 %collective-permute-done.2 = bf16[2,256,128]{2,1,0:T(8,128)(2,1)S(1)} collective-permute-done((bf16[2,256,128]{2,1,0:T(8,128)(2,1)S(1)}, bf16[2,256,128]{2,1,0:T(8,128)(2,1)S(1)}, u32[]{:S(2)}, u32[]{:S(2)}) %collective-permute-start.2) | collective-permute-done | bytes 131104 | tf_op jit(solution)/shard_map/ppermute | solution.py:14
  56.4 0.2 fusion.34
  56.8 11.2 %all_gather.3 = bf16[4,2,256,128]{3,2,1,0:T(8,128)(2,1)} all-gather(bf16[1,2,256,128]{3,2,1,0:T(8,128)(2,1)S(1)} %fusion.57), channel_id=1, replica_groups=mesh['panel'=4,'leaf'=8] {'panel'}, dimensions={0}, use_global_device_ids=true | all-gather | bytes 655360 | tf_op jit(solution)/shard_map/all_gather | solution.py:51
  68.0 1.1 %reduce_sum.12 = bf16[2,256,128]{2,1,0:T(8,128)(2,1)S(1)} reduce(bf16[4,2,256,128]{3,2,1,0:T(8,128)(2,1)} %all_gather.3, bf16[]{:T(256)} %constant.27.clone.1), dimensions={0}, to_apply=%region_0.1 | reduce | flops 196608 | bytes 655362 | tf_op jit(solution)/shard_map/reduce_sum | solution.py:50
  69.1 0.4 fusion.8
  69.5 0.4 fusion.4
  69.9 0.4 fusion.3
  70.4 0.4 fusion.2
  70.8 1.3 %pad_maximum_fusion = bf16[2,128,3072]{2,1,0:T(8,128)(2,1)} fusion(bf16[1,128,3072]{2,1,0:T(8,128)(2,1)S(1)} %fusion.2, bf16[1,128,3072]{2,1,0:T(8,128)(2,1)S(1)} %fusion.3), kind=kLoop, calls=%fused_computation.8 | loop fusion | flops 786432 | bytes 3145728 | tf_op jit(solution)/shard_map/stack | solution.py:31
  (36 shorter events, 2.9 us)
Async XLA Ops:
  0.0 3.6 %copy-start.3 = (s32[1,3072]{1,0:T(1,128)S(1)}, s32[1,3072]{1,0:T(1,128)}, u32[]{:S(2)}) copy-start(s32[1,3072]{1,0:T(1,128)} %param.6) | copy-start | bytes 36868
  30.3 1.6 %copy-start.2 = (bf16[1,128,3072]{2,1,0:T(8,128)(2,1)S(1)}, bf16[1,128,3072]{2,1,0:T(8,128)(2,1)}, u32[]{:S(2)}) copy-start(bf16[1,128,3072]{2,1,0:T(8,128)(2,1)} %copy.12) | copy-start | bytes 2359300
  32.0 4.3 %copy-start.4 = (bf16[2,256,3072]{2,1,0:T(8,128)(2,1)S(1)}, bf16[2,256,3072]{2,1,0:T(8,128)(2,1)}, u32[]{:S(2)}) copy-start(bf16[2,256,3072]{2,1,0:T(8,128)(2,1)} %param.7) | copy-start | bytes 9437188
  37.0 1.4 %copy-start.1 = (bf16[3,2,256,512]{3,2,1,0:T(8,128)(2,1)S(1)}, bf16[3,2,256,512]{3,2,1,0:T(8,128)(2,1)}, u32[]{:S(2)}) copy-start(bf16[3,2,256,512]{3,2,1,0:T(8,128)(2,1)} %param.8) | copy-start | bytes 4718596
  37.7 1.7 %collective-permute-start = (bf16[2,256,128]{1,2,0:T(8,128)(2,1)S(1)}, bf16[2,256,128]{1,2,0:T(8,128)(2,1)S(1)}, u32[]{:S(2)}, u32[]{:S(2)}) collective-permute-start(bf16[2,256,128]{1,2,0:T(8,128)(2,1)S(1)} %pad_maximum_fusion.1), channel_id=1, source_target_pairs={{0,1},{1,0},{2,3},{3,2},{4,5},{5,4},{6,7},{7,6},{8,9},{9,8},{10,11... | collective-permute-start | bytes 393224 | tf_op jit(solution)/shard_map/ppermute | solution.py:14
  40.2 6.6 %collective-permute-start.1 = (bf16[2,256,128]{2,1,0:T(8,128)(2,1)S(1)}, bf16[2,256,128]{2,1,0:T(8,128)(2,1)S(1)}, u32[]{:S(2)}, u32[]{:S(2)}) collective-permute-start(bf16[2,256,128]{2,1,0:T(8,128)(2,1)S(1)} %fusion.55), channel_id=1, source_target_pairs={{0,2},{2,0},{1,3},{3,1},{4,6},{6,4},{5,7},{7,5},{8,10},{10,8},{9,1... | collective-permute-start | bytes 393224 | tf_op jit(solution)/shard_map/ppermute | solution.py:14
  47.6 8.5 %collective-permute-start.2 = (bf16[2,256,128]{2,1,0:T(8,128)(2,1)S(1)}, bf16[2,256,128]{2,1,0:T(8,128)(2,1)S(1)}, u32[]{:S(2)}, u32[]{:S(2)}) collective-permute-start(bf16[2,256,128]{2,1,0:T(8,128)(2,1)S(1)} %fusion.56), channel_id=1, source_target_pairs={{0,4},{4,0},{1,5},{5,1},{2,6},{6,2},{3,7},{7,3},{8,12},{12,8},{9,1... | collective-permute-start | bytes 393224 | tf_op jit(solution)/shard_map/ppermute | solution.py:14
  56.2 12.9 %copy-start = (bf16[2,256,3072]{2,1,0:T(8,128)(2,1)S(1)}, bf16[2,256,3072]{2,1,0:T(8,128)(2,1)}, u32[]{:S(2)}) copy-start(bf16[2,256,3072]{2,1,0:T(8,128)(2,1)} %param.9) | copy-start | bytes 9437188
where the time goes:
time: 72.4 us; the launch traced here: 72.1 us
  local copies, waits for them, and re-layouts  21 us (29%)
  other arithmetic  13.8 us (19%)
  matrix products  11.4 us (16%)
  blocking collectives  11.2 us (15%)
  waiting for transfers between devices  7.81 us (11%)
  starting transfers between devices  6.43 us (9%)
    dot_general x32, matrix products, real_dot(): lax.dot_general(first_part, second_part, contract, preferred_element_type...  11.4 us
    all_gather x1, blocking collectives, per_device(): lax.all_gather(coefficients[None], 'panel', axis=0, tiled=True)  11.2 us
    select_n x2, other arithmetic, per_device(): gathered = jnp.take(excitation, point_order[0], axis=2)  11.1 us
    gather x1, local copies, waits for them, and re-layouts, per_device(): gathered = jnp.take(excitation, point_order[0], axis=2)  10.4 us
    ppermute x3, waiting for transfers between devices, partner_2(): return lax.ppermute(block, axis, route)  7.81 us
    ppermute x3, starting transfers between devices, partner_2(): return lax.ppermute(block, axis, route)  6.43 us
    slice x2, local copies, waits for them, and re-layouts, complex_dot(): second_matrix[1]  5.11 us
    unnamed x11, local copies, waits for them, and re-layouts  3.8 us
  transfers between devices with their start and end apart: 3, of which 2 were waited for; matrix products, arithmetic and copies ran while one was open for 3% of the time, Pallas kernels for 0%

commit v1 on v0

v1 whole, which is shorter than its diff:
```python
import functools

import jax
import jax.numpy as jnp
from jax import lax
from jax.experimental import pallas as pl
from jax.experimental.pallas import tpu as pltpu
from jax.sharding import PartitionSpec as P

MESH = pl.DeviceIdType.MESH
CHUNKS = 2
MIB = 1 << 20


def tile_of(extent, most, unit=128):
    tile = most
    while extent % tile or tile % unit:
        tile -= unit
    return tile


def combine(product, rank, width):
    real = product[:rank, :width] - product[rank:, width:]
    imag = product[:rank, width:] + product[rank:, :width]
    return jnp.concatenate((real, imag), axis=1).astype(jnp.bfloat16)


def coefficients_kernel(
    panels, leaves, levels,
    excitation_hbm, order_ref, projection_hbm, transfer_hbm, out_ref,
    excitation, projection, transfer, points, order_wide, level_zero, held, arrived, scattered, total,
    load_sem, level_send, level_recv, scatter_send, scatter_recv, gather_send, gather_recv,
):
    panel = lax.axis_index("panel")
    leaf = lax.axis_index("leaf")
    _, exc, rows = excitation.shape
    rank = projection.shape[1]
    part = exc // CHUNKS
    wide = 2 * part

    loads = [
        pltpu.make_async_copy(excitation_hbm, excitation, load_sem.at[0]),
        pltpu.make_async_copy(projection_hbm, projection, load_sem.at[1]),
        pltpu.make_async_copy(transfer_hbm, transfer, load_sem.at[2]),
    ]
    for load in loads:
        load.start()

    partners, bits = [], []
    for level in range(levels):
        span = 1 << level
        bit = lax.rem(lax.div(leaf, span), 2)
        bits.append(bit)
        partners.append(leaf + span - 2 * span * bit)
    peers = [lax.rem(panel + step, panels) for step in range(1, panels)]

    barrier = pltpu.get_barrier_semaphore()
    for partner in partners:
        pl.semaphore_signal(barrier, inc=1, device_id=(panel, partner), device_id_type=MESH)
    for peer in peers:
        pl.semaphore_signal(barrier, inc=1, device_id=(peer, leaf), device_id_type=MESH)

    for start in range(0, rows, 128):
        row = order_ref[:, start:start + 128]
        order_wide[start:start + 128, :] = jnp.broadcast_to(row, (128, 128)).T.astype(jnp.int16)

    loads[0].wait()
    source_tile = tile_of(rows, 512)
    for start in range(0, rows, source_tile):
        for chunk in range(CHUNKS):
            lanes = slice(chunk * part, (chunk + 1) * part)
            both = jnp.concatenate(
                (excitation[0, lanes, start:start + source_tile], excitation[1, lanes, start:start + source_tile]), axis=0
            )
            points[start:start + source_tile, chunk * wide:(chunk + 1) * wide] = both.T

    loads[1].wait()
    level_zero[...] = jnp.zeros_like(level_zero)
    tile = tile_of(rows, 512)

    def gather_and_project(step, carry):
        begin = pl.multiple_of(step * tile, tile)
        wanted = order_wide[pl.ds(begin, tile), :]
        lane = lax.broadcasted_iota(jnp.int32, (tile, 128), 1).astype(jnp.int16)
        one = jnp.ones((tile, 128), jnp.bfloat16)
        zero = jnp.zeros((tile, 128), jnp.bfloat16)
        chosen = jnp.concatenate(
            [jnp.where(wanted == lane + jnp.int16(start), one, zero) for start in range(0, rows, 128)], axis=1
        )
        ordered = jnp.dot(chosen, points[...], preferred_element_type=jnp.float32).astype(jnp.bfloat16)
        for side in range(2):
            level_zero[side * rank:(side + 1) * rank, :] += jnp.dot(
                projection[side, :, pl.ds(begin, tile)], ordered, preferred_element_type=jnp.float32
            )
        return carry

    lax.fori_loop(0, rows // tile, gather_and_project, 0)

    pl.semaphore_wait(barrier, levels + panels - 1)
    loads[2].wait()

    def level_copy(level, chunk):
        return pltpu.make_async_remote_copy(
            src_ref=held.at[level, chunk],
            dst_ref=arrived.at[level, chunk],
            send_sem=level_send.at[level, chunk],
            recv_sem=level_recv.at[level, chunk],
            device_id=(panel, partners[level]),
            device_id_type=MESH,
        )

    piece = rank // panels

    def scatter_copy(step, chunk):
        return pltpu.make_async_remote_copy(
            src_ref=held.at[levels, chunk, pl.ds(pl.multiple_of(peers[step] * piece, piece), piece)],
            dst_ref=scattered.at[step, chunk],
            send_sem=scatter_send.at[step, chunk],
            recv_sem=scatter_recv.at[step, chunk],
            device_id=(peers[step], leaf),
            device_id_type=MESH,
        )

    mine = pl.ds(pl.multiple_of(panel * piece, piece), piece)

    def gather_copy(step, chunk):
        return pltpu.make_async_remote_copy(
            src_ref=total.at[chunk, mine],
            dst_ref=total.at[chunk, mine],
            send_sem=gather_send.at[step, chunk],
            recv_sem=gather_recv.at[step, chunk],
            device_id=(peers[step], leaf),
            device_id_type=MESH,
        )

    def send_on(level, chunk):
        if level < levels:
            level_copy(level, chunk).start()
        else:
            for step in range(panels - 1):
                scatter_copy(step, chunk).start()

    for chunk in range(CHUNKS):
        held[0, chunk] = combine(level_zero[:, chunk * wide:(chunk + 1) * wide], rank, part)
        send_on(0, chunk)
    for level in range(levels):
        own_at = pl.ds(pl.multiple_of(bits[level] * rank, rank), rank)
        other_at = pl.ds(pl.multiple_of((1 - bits[level]) * rank, rank), rank)
        own = [
            jnp.dot(
                transfer[level, :, :, own_at].reshape(2 * rank, rank), held[level, chunk],
                preferred_element_type=jnp.float32,
            )
            for chunk in range(CHUNKS)
        ]
        for chunk in range(CHUNKS):
            level_copy(level, chunk).wait_recv()
            other = jnp.dot(
                transfer[level, :, :, other_at].reshape(2 * rank, rank), arrived[level, chunk],
                preferred_element_type=jnp.float32,
            )
            held[level + 1, chunk] = combine(own[chunk] + other, rank, part)
            send_on(level + 1, chunk)
    for chunk in range(CHUNKS):
        summed = held[levels, chunk, mine].astype(jnp.float32)
        for step in range(panels - 1):
            scatter_copy(step, chunk).wait_recv()
            summed = summed + scattered[step, chunk].astype(jnp.float32)
        total[chunk, mine] = summed.astype(jnp.bfloat16)
        for step in range(panels - 1):
            gather_copy(step, chunk).start()
    for chunk in range(CHUNKS):
        for step in range(panels - 1):
            gather_copy(step, chunk).wait_recv()
        turned = total[chunk].T
        for side in range(2):
            at = side * exc + chunk * part
            out_ref[at:at + part, :] = turned[side * part:(side + 1) * part]
    for chunk in range(CHUNKS):
        for level in range(levels):
            level_copy(level, chunk).wait_send()
        for step in range(panels - 1):
            scatter_copy(step, chunk).wait_send()
            gather_copy(step, chunk).wait_send()


def expansion_kernel(total_ref, expansion_ref, out_ref):
    exc = total_ref.shape[0] // 2
    first = jnp.dot(total_ref[...], expansion_ref[0], preferred_element_type=jnp.float32)
    second = jnp.dot(total_ref[...], expansion_ref[1], preferred_element_type=jnp.float32)
    out_ref[0] = (first[:exc] - second[exc:]).astype(out_ref.dtype)
    out_ref[1] = (second[:exc] + first[exc:]).astype(out_ref.dtype)


def per_device(excitation, point_order, projection, transfer, expansion):
    panels = lax.axis_size("panel")
    leaves = lax.axis_size("leaf")
    levels = transfer.shape[0]
    _, exc, rows = excitation.shape
    rank = projection.shape[1]
    wide = 2 * exc // CHUNKS
    total = pl.pallas_call(
        functools.partial(coefficients_kernel, panels, leaves, levels),
        out_shape=jax.ShapeDtypeStruct((2 * exc, rank), jnp.bfloat16),
        in_specs=[
            pl.BlockSpec(memory_space=pl.ANY),
            pl.BlockSpec(memory_space=pltpu.VMEM),
            pl.BlockSpec(memory_space=pl.ANY),
            pl.BlockSpec(memory_space=pl.ANY),
        ],
        out_specs=pl.BlockSpec(memory_space=pltpu.VMEM),
        scratch_shapes=[
            pltpu.VMEM(excitation.shape, jnp.bfloat16),
            pltpu.VMEM(projection.shape, jnp.bfloat16),
            pltpu.VMEM(transfer.shape, jnp.bfloat16),
            pltpu.VMEM((rows, 2 * exc), jnp.bfloat16),
            pltpu.VMEM((rows, 128), jnp.int16),
            pltpu.VMEM((2 * rank, 2 * exc), jnp.float32),
            pltpu.VMEM((levels + 1, CHUNKS, rank, wide), jnp.bfloat16),
            pltpu.VMEM((levels, CHUNKS, rank, wide), jnp.bfloat16),
            pltpu.VMEM((panels - 1, CHUNKS, rank // panels, wide), jnp.bfloat16),
            pltpu.VMEM((CHUNKS, rank, wide), jnp.bfloat16),
            pltpu.SemaphoreType.DMA((3,)),
            pltpu.SemaphoreType.DMA((levels, CHUNKS)),
            pltpu.SemaphoreType.DMA((levels, CHUNKS)),
            pltpu.SemaphoreType.DMA((panels - 1, CHUNKS)),
            pltpu.SemaphoreType.DMA((panels - 1, CHUNKS)),
            pltpu.SemaphoreType.DMA((panels - 1, CHUNKS)),
            pltpu.SemaphoreType.DMA((panels - 1, CHUNKS)),
        ],
        compiler_params=pltpu.CompilerParams(
            collective_id=0, has_side_effects=True, vmem_limit_bytes=32 * MIB
        ),
    )(excitation, point_order, projection, transfer)
    columns = tile_of(rows, 1024)
    return pl.pallas_call(
        expansion_kernel,
        out_shape=jax.ShapeDtypeStruct((2, exc, rows), jnp.bfloat16),
        grid=(rows // columns,),
        in_specs=[
            pl.BlockSpec((2 * exc, rank), lambda step: (0, 0)),
            pl.BlockSpec((2, rank, columns), lambda step: (0, 0, step)),
        ],
        out_specs=pl.BlockSpec((2, exc, columns), lambda step: (0, 0, step)),
        compiler_params=pltpu.CompilerParams(vmem_limit_bytes=16 * MIB),
    )(total, expansion)


def solution(mesh):
    in_specs = (
        P(None, None, ("panel", "leaf")),
        P(("panel", "leaf"), None),
        P(None, None, ("panel", "leaf")),
        P(None, None, ("panel", "leaf"), None),
        P(None, None, ("panel", "leaf")),
    )
    out_specs = P(None, None, ("panel", "leaf"))
    return jax.shard_map(
        per_device, mesh=mesh, in_specs=in_specs, out_specs=out_specs, check_vma=False
    )
```

time: 72.4 us -> 42.8 us (0.59)
  Pallas kernels: 0 us -> 37.2 us
  local copies, waits for them, and re-layouts: 21 us -> 5.41 us
  other arithmetic: 13.8 us -> 0 us
  matrix products: 11.4 us -> 0 us
  blocking collectives: 11.2 us -> 0 us
  waiting for transfers between devices: 7.81 us -> 0 us
  starting transfers between devices: 6.43 us -> 0 us
    pallas_call x0 -> x2, Pallas kernels: none -> 37.2 us  [the longest x1 34.5 us: per_device(): pl.pallas_call(functools.partial(coefficients_kernel, panels, leaves, lev...]
    dot_general x32 -> x0, matrix products: 11.4 us -> none  [real_dot(): lax.dot_general(first_part, second_part, contract, preferred_element_type...]
    select_n x5 -> x0, other arithmetic: 11.3 us -> none  [the longest x2 11.1 us: per_device(): gathered = jnp.take(excitation, point_order[0], axis=2)]
    all_gather x1 -> x0, blocking collectives: 11.2 us -> none  [per_device(): lax.all_gather(coefficients[None], 'panel', axis=0, tiled=True)]
    gather x1 -> x0, local copies, waits for them, and re-layouts: 10.4 us -> none  [per_device(): gathered = jnp.take(excitation, point_order[0], axis=2)]
    ppermute x3 -> x0, waiting for transfers between devices: 7.81 us -> none  [partner_2(): return lax.ppermute(block, axis, route)]
    slice x3 -> x0, local copies, waits for them, and re-layouts: 6.72 us -> none  [the longest x2 5.11 us: complex_dot(): second_matrix[1]]
    ppermute x3 -> x0, starting transfers between devices: 6.43 us -> none  [partner_2(): return lax.ppermute(block, axis, route)]
  transfers between devices with their start and end apart: 3 -> 0, of which waited for: 2 -> 0; matrix products, arithmetic and copies ran while one was open for 3% -> 0% of each run, Pallas kernels for 0% -> 0%
where the time goes in v1:
time: 42.8 us; the launch traced here: 42.6 us
  Pallas kernels  37.2 us (87%)
  local copies, waits for them, and re-layouts  5.41 us (13%)
    pallas_call x1, Pallas kernels, per_device(): pl.pallas_call(functools.partial(coefficients_kernel, panels, leaves, lev...  34.5 us
    unnamed x10, local copies, waits for them, and re-layouts  5.41 us
    pallas_call x1, Pallas kernels, per_device(): pl.pallas_call(expansion_kernel, out_shape=jax.ShapeDtypeStruct((2, exc,...  2.65 us

profile of v1, /device:TPU:0, one launch (start us, length us, event | category | flops | bytes accessed | tf_op | source)
XLA Modules:
  0.0 42.6 jit_solution(11369715747827971354)
XLA Ops:
  0.0 0.0 copy-start.1
  0.0 1.9 %copy-done.1 = bf16[2,256,3072]{2,1,0:T(8,128)(2,1)S(1)} copy-done((bf16[2,256,3072]{2,1,0:T(8,128)(2,1)S(1)}, bf16[2,256,3072]{2,1,0:T(8,128)(2,1)}, u32[]{:S(2)}) %copy-start.1) | copy-done | bytes 3145752
  1.9 0.0 copy-start.2
  1.9 1.4 %copy-done.2 = bf16[2,128,3072]{2,1,0:T(8,128)(2,1)S(1)} copy-done((bf16[2,128,3072]{2,1,0:T(8,128)(2,1)S(1)}, bf16[2,128,3072]{2,1,0:T(8,128)(2,1)}, u32[]{:S(2)}) %copy-start.2) | copy-done | bytes 1572888
  3.3 0.0 copy-start.3
  3.3 1.4 %copy-done.3 = bf16[3,2,256,512]{3,2,1,0:T(8,128)(2,1)S(1)} copy-done((bf16[3,2,256,512]{3,2,1,0:T(8,128)(2,1)S(1)}, bf16[3,2,256,512]{3,2,1,0:T(8,128)(2,1)}, u32[]{:S(2)}) %copy-start.3) | copy-done | bytes 1572888
  4.7 0.0 copy-start.4
  4.7 0.7 %copy-done.4 = s32[1,3072]{1,0:T(1,128)S(1)} copy-done((s32[1,3072]{1,0:T(1,128)S(1)}, s32[1,3072]{1,0:T(1,128)}, u32[]{:S(2)}) %copy-start.4) | copy-done | bytes 12312
  5.4 0.0 copy-start
  5.4 34.5 %shard_map.55.total_ref = bf16[256,256]{1,0:T(8,128)(2,1)S(1)} custom-call(bf16[2,128,3072]{2,1,0:T(8,128)(2,1)S(1)} %copy-done.2, s32[1,3072]{1,0:T(1,128)S(1)} %copy-done.4, bf16[2,256,3072]{2,1,0:T(8,128)(2,1)S(1)} %copy-done.1, bf16[3,2,256,512]{3,2,1,0:T(8,128)(2,1)S(1)} %copy-done.3), custom_call_target="tpu_custom_call" | custom-call | tf_op jit(solution)/shard_map/pallas_call | solution.py:202
  39.9 0.0 copy-done
  39.9 2.6 %shard_map.56 = bf16[2,128,3072]{2,1,0:T(8,128)(2,1)} custom-call(bf16[256,256]{1,0:T(8,128)(2,1)S(1)} %shard_map.55.total_ref, bf16[2,256,3072]{2,1,0:T(8,128)(2,1)S(1)} %copy-done), custom_call_target="tpu_custom_call" | custom-call | tf_op jit(solution)/shard_map/pallas_call | solution.py:236
Async XLA Ops:
  0.0 1.9 %copy-start.1 = (bf16[2,256,3072]{2,1,0:T(8,128)(2,1)S(1)}, bf16[2,256,3072]{2,1,0:T(8,128)(2,1)}, u32[]{:S(2)}) copy-start(bf16[2,256,3072]{2,1,0:T(8,128)(2,1)} %projection_hbm.1) | copy-start | bytes 9437188
  1.9 1.4 %copy-start.2 = (bf16[2,128,3072]{2,1,0:T(8,128)(2,1)S(1)}, bf16[2,128,3072]{2,1,0:T(8,128)(2,1)}, u32[]{:S(2)}) copy-start(bf16[2,128,3072]{2,1,0:T(8,128)(2,1)} %excitation_hbm.1) | copy-start | bytes 4718596
  3.3 1.4 %copy-start.3 = (bf16[3,2,256,512]{3,2,1,0:T(8,128)(2,1)S(1)}, bf16[3,2,256,512]{3,2,1,0:T(8,128)(2,1)}, u32[]{:S(2)}) copy-start(bf16[3,2,256,512]{3,2,1,0:T(8,128)(2,1)} %transfer_hbm.1) | copy-start | bytes 4718596
  4.7 0.7 %copy-start.4 = (s32[1,3072]{1,0:T(1,128)S(1)}, s32[1,3072]{1,0:T(1,128)}, u32[]{:S(2)}) copy-start(s32[1,3072]{1,0:T(1,128)} %order_ref.1) | copy-start | bytes 36868
  5.4 34.5 %copy-start = (bf16[2,256,3072]{2,1,0:T(8,128)(2,1)S(1)}, bf16[2,256,3072]{2,1,0:T(8,128)(2,1)}, u32[]{:S(2)}) copy-start(bf16[2,256,3072]{2,1,0:T(8,128)(2,1)} %expansion_ref.1) | copy-start | bytes 9437188

commit v2 on v1

v2 whole, which is shorter than its diff:
```python
import functools

import jax
import jax.numpy as jnp
from jax import lax
from jax.experimental import pallas as pl
from jax.experimental.pallas import tpu as pltpu
from jax.sharding import PartitionSpec as P

MESH = pl.DeviceIdType.MESH
CHUNKS = 2
MIB = 1 << 20


def tile_of(extent, most, unit=128):
    tile = most
    while extent % tile or tile % unit:
        tile -= unit
    return tile


def combine(product, rank, width):
    real = product[:rank, :width] - product[rank:, width:]
    imag = product[:rank, width:] + product[rank:, :width]
    return jnp.concatenate((real, imag), axis=1).astype(jnp.bfloat16)


def coefficients_kernel(
    panels, levels,
    excitation_hbm, order_hbm, projection_hbm, transfer_hbm, out_ref,
    excitation, order, projection, transfer, crossing, points, order_wide, ordered,
    held, arrived, partial, scattered, cross_out, cross_in, total,
    load_sem, matrix_sem, level_send, level_recv, scatter_send, scatter_recv,
    cross_send, cross_recv, gather_send, gather_recv,
):
    panel = lax.axis_index("panel")
    leaf = lax.axis_index("leaf")
    _, exc, rows = excitation_hbm.shape
    rank = projection.shape[1]
    part = exc // CHUNKS
    wide = 2 * part
    top = levels - 1

    loads = [pltpu.make_async_copy(order_hbm, order, load_sem.at[0])]
    for chunk in range(CHUNKS):
        for side in range(2):
            at = chunk * wide + side * part
            loads.append(
                pltpu.make_async_copy(
                    excitation_hbm.at[side, pl.ds(chunk * part, part)], excitation.at[pl.ds(at, part)],
                    load_sem.at[3 + 2 * chunk + side],
                )
            )
    projection_load = pltpu.make_async_copy(projection_hbm, projection, load_sem.at[1])
    transfer_load = pltpu.make_async_copy(transfer_hbm, transfer, load_sem.at[2])
    for load in loads:
        load.start()
    projection_load.start()
    transfer_load.start()

    partners, bits = [], []
    for level in range(levels):
        span = 1 << level
        bit = lax.rem(lax.div(leaf, span), 2)
        bits.append(bit)
        partners.append(leaf + span - 2 * span * bit)
    peers = [lax.rem(panel + step, panels) for step in range(1, panels)]
    own_at = [pl.ds(pl.multiple_of(bit * rank, rank), rank) for bit in bits]
    other_at = [pl.ds(pl.multiple_of((1 - bit) * rank, rank), rank) for bit in bits]

    barrier = pltpu.get_barrier_semaphore()
    for partner in partners:
        pl.semaphore_signal(barrier, inc=1, device_id=(panel, partner), device_id_type=MESH)
    for peer in peers:
        pl.semaphore_signal(barrier, inc=1, device_id=(peer, leaf), device_id_type=MESH)

    loads[0].wait()
    for start in range(0, rows, 128):
        row = order[:, start:start + 128]
        order_wide[start:start + 128, :] = jnp.broadcast_to(row, (128, 128)).T.astype(jnp.int16)
    for load in loads[1:]:
        load.wait()

    pl.semaphore_wait(barrier, levels + panels - 1)
    matrix_copy = pltpu.make_async_remote_copy(
        src_ref=transfer_hbm.at[top, :, :, other_at[top]],
        dst_ref=crossing,
        send_sem=matrix_sem.at[0],
        recv_sem=matrix_sem.at[1],
        device_id=(panel, partners[top]),
        device_id_type=MESH,
    )
    matrix_copy.start()

    source_tile = tile_of(rows, 512)
    for start in range(0, rows, source_tile):
        points[start:start + source_tile, :] = excitation[:, start:start + source_tile].T

    tile = tile_of(rows, 512)
    lane = lax.broadcasted_iota(jnp.int32, (tile, 128), 1).astype(jnp.int16)
    one = jnp.ones((tile, 128), jnp.bfloat16)
    zero = jnp.zeros((tile, 128), jnp.bfloat16)
    for begin in range(0, rows, tile):
        wanted = order_wide[begin:begin + tile, :]
        chosen = jnp.concatenate(
            [jnp.where(wanted == lane + jnp.int16(start), one, zero) for start in range(0, rows, 128)], axis=1
        )
        ordered[begin:begin + tile, :] = jnp.dot(
            chosen, points[...], preferred_element_type=jnp.float32
        ).astype(jnp.bfloat16)

    projection_load.wait()
    level_zero = jnp.dot(
        projection[...].reshape(2 * rank, rows), ordered[...], preferred_element_type=jnp.float32
    )

    def level_copy(level, chunk):
        return pltpu.make_async_remote_copy(
            src_ref=held.at[level, chunk],
            dst_ref=arrived.at[level, chunk],
            send_sem=level_send.at[level, chunk],
            recv_sem=level_recv.at[level, chunk],
            device_id=(panel, partners[level]),
            device_id_type=MESH,
        )

    piece = rank // panels

    def scatter_copy(step, chunk):
        return pltpu.make_async_remote_copy(
            src_ref=partial.at[chunk, :, pl.ds(pl.multiple_of(peers[step] * piece, piece), piece)],
            dst_ref=scattered.at[step, chunk],
            send_sem=scatter_send.at[step, chunk],
            recv_sem=scatter_recv.at[step, chunk],
            device_id=(peers[step], leaf),
            device_id_type=MESH,
        )

    def cross_copy(chunk):
        return pltpu.make_async_remote_copy(
            src_ref=cross_out.at[chunk],
            dst_ref=cross_in.at[chunk],
            send_sem=cross_send.at[chunk],
            recv_sem=cross_recv.at[chunk],
            device_id=(panel, partners[top]),
            device_id_type=MESH,
        )

    mine = pl.ds(pl.multiple_of(panel * piece, piece), piece)

    def gather_copy(step, chunk):
        return pltpu.make_async_remote_copy(
            src_ref=total.at[chunk, mine],
            dst_ref=total.at[chunk, mine],
            send_sem=gather_send.at[step, chunk],
            recv_sem=gather_recv.at[step, chunk],
            device_id=(peers[step], leaf),
            device_id_type=MESH,
        )

    def product(matrix, block):
        return jnp.dot(matrix.reshape(2 * rank, rank), block, preferred_element_type=jnp.float32)

    for chunk in range(CHUNKS):
        held[0, chunk] = combine(level_zero[:, chunk * wide:(chunk + 1) * wide], rank, part)
        if top > 0:
            level_copy(0, chunk).start()
    transfer_load.wait()
    for level in range(top):
        own = [product(transfer[level, :, :, own_at[level]], held[level, chunk]) for chunk in range(CHUNKS)]
        for chunk in range(CHUNKS):
            level_copy(level, chunk).wait_recv()
            other = product(transfer[level, :, :, other_at[level]], arrived[level, chunk])
            held[level + 1, chunk] = combine(own[chunk] + other, rank, part)
            if level + 1 < top:
                level_copy(level + 1, chunk).start()
            else:
                if chunk == 0:
                    matrix_copy.wait_recv()
                partial[chunk, 0] = combine(
                    product(transfer[top, :, :, own_at[top]], held[top, chunk]), rank, part
                )
                partial[chunk, 1] = combine(product(crossing[...], held[top, chunk]), rank, part)
                for step in range(panels - 1):
                    scatter_copy(step, chunk).start()
    kept = []
    for chunk in range(CHUNKS):
        sums = [partial[chunk, side, mine].astype(jnp.float32) for side in range(2)]
        for step in range(panels - 1):
            scatter_copy(step, chunk).wait_recv()
            sums = [sums[side] + scattered[step, chunk, side].astype(jnp.float32) for side in range(2)]
        cross_out[chunk] = sums[1].astype(jnp.bfloat16)
        cross_copy(chunk).start()
        kept.append(sums[0])
    for chunk in range(CHUNKS):
        cross_copy(chunk).wait_recv()
        total[chunk, mine] = (kept[chunk] + cross_in[chunk].astype(jnp.float32)).astype(jnp.bfloat16)
        for step in range(panels - 1):
            gather_copy(step, chunk).start()
    for chunk in range(CHUNKS):
        for step in range(panels - 1):
            gather_copy(step, chunk).wait_recv()
        turned = total[chunk].T
        for side in range(2):
            at = side * exc + chunk * part
            out_ref[at:at + part, :] = turned[side * part:(side + 1) * part]
    matrix_copy.wait_send()
    for chunk in range(CHUNKS):
        for level in range(top):
            level_copy(level, chunk).wait_send()
        cross_copy(chunk).wait_send()
        for step in range(panels - 1):
            scatter_copy(step, chunk).wait_send()
            gather_copy(step, chunk).wait_send()


def expansion_kernel(total_hbm, expansion_ref, out_hbm, total_ref, out, load_sem, store_sem):
    load = pltpu.make_async_copy(total_hbm, total_ref, load_sem)
    load.start()
    load.wait()
    exc = total_ref.shape[0] // 2
    rows = expansion_ref.shape[2]
    columns = tile_of(rows, 768)
    stores = []
    for step in range(rows // columns):
        span = slice(step * columns, (step + 1) * columns)
        first = jnp.dot(total_ref[...], expansion_ref[0, :, span], preferred_element_type=jnp.float32)
        second = jnp.dot(total_ref[...], expansion_ref[1, :, span], preferred_element_type=jnp.float32)
        out[0, :, span] = (first[:exc] - second[exc:]).astype(out.dtype)
        out[1, :, span] = (second[:exc] + first[exc:]).astype(out.dtype)
        at = pl.ds(step * columns, columns)
        store = pltpu.make_async_copy(out.at[:, :, at], out_hbm.at[:, :, at], store_sem.at[step])
        store.start()
        stores.append(store)
    for store in stores:
        store.wait()


def per_device(excitation, point_order, projection, transfer, expansion):
    panels = lax.axis_size("panel")
    levels = transfer.shape[0]
    _, exc, rows = excitation.shape
    rank = projection.shape[1]
    wide = 2 * exc // CHUNKS
    piece = rank // panels
    total = pl.pallas_call(
        functools.partial(coefficients_kernel, panels, levels),
        out_shape=jax.ShapeDtypeStruct((2 * exc, rank), jnp.bfloat16),
        in_specs=[pl.BlockSpec(memory_space=pl.ANY)] * 4,
        out_specs=pl.BlockSpec(memory_space=pltpu.VMEM),
        scratch_shapes=[
            pltpu.VMEM((2 * exc, rows), jnp.bfloat16),
            pltpu.VMEM((1, rows), jnp.int32),
            pltpu.VMEM(projection.shape, jnp.bfloat16),
            pltpu.VMEM(transfer.shape, jnp.bfloat16),
            pltpu.VMEM((2, rank, rank), jnp.bfloat16),
            pltpu.VMEM((rows, 2 * exc), jnp.bfloat16),
            pltpu.VMEM((rows, 128), jnp.int16),
            pltpu.VMEM((rows, 2 * exc), jnp.bfloat16),
            pltpu.VMEM((levels, CHUNKS, rank, wide), jnp.bfloat16),
            pltpu.VMEM((levels, CHUNKS, rank, wide), jnp.bfloat16),
            pltpu.VMEM((CHUNKS, 2, rank, wide), jnp.bfloat16),
            pltpu.VMEM((panels - 1, CHUNKS, 2, piece, wide), jnp.bfloat16),
            pltpu.VMEM((CHUNKS, piece, wide), jnp.bfloat16),
            pltpu.VMEM((CHUNKS, piece, wide), jnp.bfloat16),
            pltpu.VMEM((CHUNKS, rank, wide), jnp.bfloat16),
            pltpu.SemaphoreType.DMA((3 + 2 * CHUNKS,)),
            pltpu.SemaphoreType.DMA((2,)),
            pltpu.SemaphoreType.DMA((levels, CHUNKS)),
            pltpu.SemaphoreType.DMA((levels, CHUNKS)),
            pltpu.SemaphoreType.DMA((panels - 1, CHUNKS)),
            pltpu.SemaphoreType.DMA((panels - 1, CHUNKS)),
            pltpu.SemaphoreType.DMA((CHUNKS,)),
            pltpu.SemaphoreType.DMA((CHUNKS,)),
            pltpu.SemaphoreType.DMA((panels - 1, CHUNKS)),
            pltpu.SemaphoreType.DMA((panels - 1, CHUNKS)),
        ],
        compiler_params=pltpu.CompilerParams(
            collective_id=0, has_side_effects=True, vmem_limit_bytes=60 * MIB
        ),
    )(excitation, point_order, projection, transfer)
    return pl.pallas_call(
        expansion_kernel,
        out_shape=jax.ShapeDtypeStruct((2, exc, rows), jnp.bfloat16),
        in_specs=[pl.BlockSpec(memory_space=pl.ANY), pl.BlockSpec(memory_space=pltpu.VMEM)],
        out_specs=pl.BlockSpec(memory_space=pl.ANY),
        scratch_shapes=[
            pltpu.VMEM((2 * exc, rank), jnp.bfloat16),
            pltpu.VMEM((2, exc, rows), jnp.bfloat16),
            pltpu.SemaphoreType.DMA,
            pltpu.SemaphoreType.DMA((rows // tile_of(rows, 768),)),
        ],
        compiler_params=pltpu.CompilerParams(vmem_limit_bytes=60 * MIB),
    )(total, expansion)


def solution(mesh):
    in_specs = (
        P(None, None, ("panel", "leaf")),
        P(("panel", "leaf"), None),
        P(None, None, ("panel", "leaf")),
        P(None, None, ("panel", "leaf"), None),
        P(None, None, ("panel", "leaf")),
    )
    out_specs = P(None, None, ("panel", "leaf"))
    return jax.shard_map(
        per_device, mesh=mesh, in_specs=in_specs, out_specs=out_specs, check_vma=False
    )
```

time: 42.8 us -> 36.1 us (0.84)
  local copies, waits for them, and re-layouts: 5.41 us -> 0 us
  Pallas kernels: 37.2 us -> 35.9 us
    unnamed x10 -> x0, local copies, waits for them, and re-layouts: 5.41 us -> none
    pallas_call x1, Pallas kernels: 34.5 us -> 31.3 us  [per_device(): pl.pallas_call(functools.partial(coefficients_kernel, panels, levels), ou...]
    pallas_call x1, Pallas kernels: 2.65 us -> 4.57 us  [per_device(): pl.pallas_call(expansion_kernel, out_shape=jax.ShapeDtypeStruct((2, exc,...]
where the time goes in v2:
time: 36.1 us; the launch traced here: 35.9 us
  Pallas kernels  35.9 us (99%)
    pallas_call x1, Pallas kernels, per_device(): pl.pallas_call(functools.partial(coefficients_kernel, panels, levels), ou...  31.3 us
    pallas_call x1, Pallas kernels, per_device(): pl.pallas_call(expansion_kernel, out_shape=jax.ShapeDtypeStruct((2, exc,...  4.57 us

profile of v2, /device:TPU:0, one launch (start us, length us, event | category | flops | bytes accessed | tf_op | source)
XLA Modules:
  0.0 35.9 jit_solution(6204764775826817323)
XLA Ops:
  0.0 31.3 %shard_map.55.total_hbm = bf16[256,256]{1,0:T(8,128)(2,1)} custom-call(bf16[2,128,3072]{2,1,0:T(8,128)(2,1)} %excitation_hbm.1, s32[1,3072]{1,0:T(1,128)} %order_hbm.1, bf16[2,256,3072]{2,1,0:T(8,128)(2,1)} %projection_hbm.1, bf16[3,2,256,512]{3,2,1,0:T(8,128)(2,1)} %transfer_hbm.1), custom_call_target="tpu_custom_call" | custom-call | tf_op jit(solution)/shard_map/pallas_call | solution.py:246
  31.3 4.6 %shard_map.56 = bf16[2,128,3072]{2,1,0:T(8,128)(2,1)} custom-call(bf16[256,256]{1,0:T(8,128)(2,1)} %shard_map.55.total_hbm, bf16[2,256,3072]{2,1,0:T(8,128)(2,1)} %expansion_ref.1), custom_call_target="tpu_custom_call" | custom-call | tf_op jit(solution)/shard_map/pallas_call | solution.py:282

commit v3 on v2

--- a/solution.py
+++ b/solution.py
@@ -9,6 +9,7 @@
 
 MESH = pl.DeviceIdType.MESH
 CHUNKS = 2
+GROUP = 16
 MIB = 1 << 20
 
 
@@ -28,7 +29,7 @@
 def coefficients_kernel(
     panels, levels,
     excitation_hbm, order_hbm, projection_hbm, transfer_hbm, out_ref,
-    excitation, order, projection, transfer, crossing, points, order_wide, ordered,
+    excitation, order, order_scalar, projection, transfer, crossing, points, points_wide, picked, order_wide, ordered,
     held, arrived, partial, scattered, cross_out, cross_in, total,
     load_sem, matrix_sem, level_send, level_recv, scatter_send, scatter_recv,
     cross_send, cross_recv, gather_send, gather_recv,
@@ -51,10 +52,12 @@
                     load_sem.at[3 + 2 * chunk + side],
                 )
             )
+    scalar_load = pltpu.make_async_copy(order_hbm, order_scalar, load_sem.at[3 + 2 * CHUNKS])
     projection_load = pltpu.make_async_copy(projection_hbm, projection, load_sem.at[1])
     transfer_load = pltpu.make_async_copy(transfer_hbm, transfer, load_sem.at[2])
     for load in loads:
         load.start()
+    scalar_load.start()
     projection_load.start()
     transfer_load.start()
 
@@ -94,20 +97,36 @@
 
     source_tile = tile_of(rows, 512)
     for start in range(0, rows, source_tile):
-        points[start:start + source_tile, :] = excitation[:, start:start + source_tile].T
+        turned = excitation[:, start:start + source_tile].T
+        points[start:start + source_tile, :] = turned
+        points_wide[start:start + source_tile, :] = turned.astype(jnp.float32)
+    scalar_load.wait()
 
     tile = tile_of(rows, 512)
-    lane = lax.broadcasted_iota(jnp.int32, (tile, 128), 1).astype(jnp.int16)
-    one = jnp.ones((tile, 128), jnp.bfloat16)
-    zero = jnp.zeros((tile, 128), jnp.bfloat16)
-    for begin in range(0, rows, tile):
-        wanted = order_wide[begin:begin + tile, :]
+    read = picked.shape[0]
+
+    def gather(step, carry):
+        begin = pl.multiple_of(step * tile, tile)
+        for base in range(0, read, GROUP):
+            found = [
+                points_wide[pl.ds(order_scalar[0, begin + base + row], 1), :] for row in range(GROUP)
+            ]
+            for row in range(GROUP):
+                picked[base + row:base + row + 1, :] = found[row]
+        wanted = order_wide[pl.ds(begin + read, tile - read), :]
+        lane = lax.broadcasted_iota(jnp.int32, wanted.shape, 1).astype(jnp.int16)
+        one = jnp.ones(wanted.shape, jnp.bfloat16)
+        zero = jnp.zeros(wanted.shape, jnp.bfloat16)
         chosen = jnp.concatenate(
             [jnp.where(wanted == lane + jnp.int16(start), one, zero) for start in range(0, rows, 128)], axis=1
         )
-        ordered[begin:begin + tile, :] = jnp.dot(
+        ordered[pl.ds(begin + read, tile - read), :] = jnp.dot(
             chosen, points[...], preferred_element_type=jnp.float32
         ).astype(jnp.bfloat16)
+        ordered[pl.ds(begin, read), :] = picked[...].astype(jnp.bfloat16)
+        return carry
+
+    lax.fori_loop(0, rows // tile, gather, 0)
 
     projection_load.wait()
     level_zero = jnp.dot(
@@ -251,10 +270,13 @@
         scratch_shapes=[
             pltpu.VMEM((2 * exc, rows), jnp.bfloat16),
             pltpu.VMEM((1, rows), jnp.int32),
+            pltpu.SMEM((1, rows), jnp.int32),
             pltpu.VMEM(projection.shape, jnp.bfloat16),
             pltpu.VMEM(transfer.shape, jnp.bfloat16),
             pltpu.VMEM((2, rank, rank), jnp.bfloat16),
             pltpu.VMEM((rows, 2 * exc), jnp.bfloat16),
+            pltpu.VMEM((rows, 2 * exc), jnp.float32),
+            pltpu.VMEM((tile_of(rows, 512) // 2, 2 * exc), jnp.float32),
             pltpu.VMEM((rows, 128), jnp.int16),
             pltpu.VMEM((rows, 2 * exc), jnp.bfloat16),
             pltpu.VMEM((levels, CHUNKS, rank, wide), jnp.bfloat16),
@@ -264,7 +286,7 @@
             pltpu.VMEM((CHUNKS, piece, wide), jnp.bfloat16),
             pltpu.VMEM((CHUNKS, piece, wide), jnp.bfloat16),
             pltpu.VMEM((CHUNKS, rank, wide), jnp.bfloat16),
-            pltpu.SemaphoreType.DMA((3 + 2 * CHUNKS,)),
+            pltpu.SemaphoreType.DMA((4 + 2 * CHUNKS,)),
             pltpu.SemaphoreType.DMA((2,)),
             pltpu.SemaphoreType.DMA((levels, CHUNKS)),
             pltpu.SemaphoreType.DMA((levels, CHUNKS)),
@@ -290,7 +312,7 @@
             pltpu.SemaphoreType.DMA,
             pltpu.SemaphoreType.DMA((rows // tile_of(rows, 768),)),
         ],
-        compiler_params=pltpu.CompilerParams(vmem_limit_bytes=60 * MIB),
+        compiler_params=pltpu.CompilerParams(vmem_limit_bytes=24 * MIB),
     )(total, expansion)
 
 

time: 36.1 us -> 35.9 us (level)
  Pallas kernels: 35.9 us -> 34.8 us
  local copies, waits for them, and re-layouts: 0 us -> 0.9 us
    pallas_call x1, Pallas kernels: 4.57 us -> 1.91 us  [per_device(): pl.pallas_call(expansion_kernel, out_shape=jax.ShapeDtypeStruct((2, exc,...]
    pallas_call x1, Pallas kernels: 31.3 us -> 32.9 us  [per_device(): pl.pallas_call(functools.partial(coefficients_kernel, panels, levels), ou...]
    unnamed x0 -> x4, local copies, waits for them, and re-layouts: none -> 0.9 us
where the time goes in v3:
time: 35.9 us; the launch traced here: 35.7 us
  Pallas kernels  34.8 us (97%)
  local copies, waits for them, and re-layouts  0.9 us (3%)
    pallas_call x1, Pallas kernels, per_device(): pl.pallas_call(functools.partial(coefficients_kernel, panels, levels), ou...  32.9 us
    pallas_call x1, Pallas kernels, per_device(): pl.pallas_call(expansion_kernel, out_shape=jax.ShapeDtypeStruct((2, exc,...  1.91 us
    unnamed x4, local copies, waits for them, and re-layouts  0.9 us

profile of v3, /device:TPU:0, one launch (start us, length us, event | category | flops | bytes accessed | tf_op | source)
XLA Modules:
  0.0 35.7 jit_solution(1171747460206883874)
XLA Ops:
  0.0 0.0 copy-start
  0.0 32.9 %shard_map.55.total_hbm = bf16[256,256]{1,0:T(8,128)(2,1)} custom-call(bf16[2,128,3072]{2,1,0:T(8,128)(2,1)} %excitation_hbm.1, s32[1,3072]{1,0:T(1,128)} %order_hbm.1, bf16[2,256,3072]{2,1,0:T(8,128)(2,1)} %projection_hbm.1, bf16[3,2,256,512]{3,2,1,0:T(8,128)(2,1)} %transfer_hbm.1), custom_call_target="tpu_custom_call" | custom-call | tf_op jit(solution)/shard_map/pallas_call | solution.py:265
  32.9 0.0 copy-done
  32.9 0.0 copy-start.1
  32.9 0.9 %copy-done.1 = bf16[256,256]{1,0:T(8,128)(2,1)S(1)} copy-done((bf16[256,256]{1,0:T(8,128)(2,1)S(1)}, bf16[256,256]{1,0:T(8,128)(2,1)}, u32[]{:S(2)}) %copy-start.1) | copy-done | bytes 131096
  33.8 1.9 %shard_map.56 = bf16[2,128,3072]{2,1,0:T(8,128)(2,1)} custom-call(bf16[256,256]{1,0:T(8,128)(2,1)S(1)} %copy-done.1, bf16[2,256,3072]{2,1,0:T(8,128)(2,1)S(1)} %copy-done), custom_call_target="tpu_custom_call" | custom-call | tf_op jit(solution)/shard_map/pallas_call | solution.py:304
Async XLA Ops:
  0.0 32.9 %copy-start = (bf16[2,256,3072]{2,1,0:T(8,128)(2,1)S(1)}, bf16[2,256,3072]{2,1,0:T(8,128)(2,1)}, u32[]{:S(2)}) copy-start(bf16[2,256,3072]{2,1,0:T(8,128)(2,1)} %expansion_ref.1) | copy-start | bytes 9437188
  32.9 0.9 %copy-start.1 = (bf16[256,256]{1,0:T(8,128)(2,1)S(1)}, bf16[256,256]{1,0:T(8,128)(2,1)}, u32[]{:S(2)}) copy-start(bf16[256,256]{1,0:T(8,128)(2,1)} %shard_map.55.total_hbm) | copy-start | bytes 393220

commit v4 on v2

--- a/solution.py
+++ b/solution.py
@@ -290,7 +290,7 @@
             pltpu.SemaphoreType.DMA,
             pltpu.SemaphoreType.DMA((rows // tile_of(rows, 768),)),
         ],
-        compiler_params=pltpu.CompilerParams(vmem_limit_bytes=60 * MIB),
+        compiler_params=pltpu.CompilerParams(vmem_limit_bytes=24 * MIB),
     )(total, expansion)
 
 

time: 36.1 us -> 34.3 us (0.950)
  Pallas kernels: 35.9 us -> 33.2 us
  local copies, waits for them, and re-layouts: 0 us -> 0.9 us
    pallas_call x1, Pallas kernels: 4.57 us -> 1.91 us  [per_device(): pl.pallas_call(expansion_kernel, out_shape=jax.ShapeDtypeStruct((2, exc,...]
    unnamed x0 -> x4, local copies, waits for them, and re-layouts: none -> 0.9 us
where the time goes in v4:
time: 34.3 us; the launch traced here: 34.2 us
  Pallas kernels  33.2 us (97%)
  local copies, waits for them, and re-layouts  0.9 us (3%)
    pallas_call x1, Pallas kernels, per_device(): pl.pallas_call(functools.partial(coefficients_kernel, panels, levels), ou...  31.3 us
    pallas_call x1, Pallas kernels, per_device(): pl.pallas_call(expansion_kernel, out_shape=jax.ShapeDtypeStruct((2, exc,...  1.91 us
    unnamed x4, local copies, waits for them, and re-layouts  0.9 us

profile of v4, /device:TPU:0, one launch (start us, length us, event | category | flops | bytes accessed | tf_op | source)
XLA Modules:
  0.0 34.2 jit_solution(14923370866309968645)
XLA Ops:
  0.0 0.0 copy-start
  0.0 31.3 %shard_map.55.total_hbm = bf16[256,256]{1,0:T(8,128)(2,1)} custom-call(bf16[2,128,3072]{2,1,0:T(8,128)(2,1)} %excitation_hbm.1, s32[1,3072]{1,0:T(1,128)} %order_hbm.1, bf16[2,256,3072]{2,1,0:T(8,128)(2,1)} %projection_hbm.1, bf16[3,2,256,512]{3,2,1,0:T(8,128)(2,1)} %transfer_hbm.1), custom_call_target="tpu_custom_call" | custom-call | tf_op jit(solution)/shard_map/pallas_call | solution.py:246
  31.3 0.0 copy-done
  31.3 0.0 copy-start.1
  31.3 0.9 %copy-done.1 = bf16[256,256]{1,0:T(8,128)(2,1)S(1)} copy-done((bf16[256,256]{1,0:T(8,128)(2,1)S(1)}, bf16[256,256]{1,0:T(8,128)(2,1)}, u32[]{:S(2)}) %copy-start.1) | copy-done | bytes 131096
  32.2 1.9 %shard_map.56 = bf16[2,128,3072]{2,1,0:T(8,128)(2,1)} custom-call(bf16[256,256]{1,0:T(8,128)(2,1)S(1)} %copy-done.1, bf16[2,256,3072]{2,1,0:T(8,128)(2,1)S(1)} %copy-done), custom_call_target="tpu_custom_call" | custom-call | tf_op jit(solution)/shard_map/pallas_call | solution.py:282
Async XLA Ops:
  0.0 31.3 %copy-start = (bf16[2,256,3072]{2,1,0:T(8,128)(2,1)S(1)}, bf16[2,256,3072]{2,1,0:T(8,128)(2,1)}, u32[]{:S(2)}) copy-start(bf16[2,256,3072]{2,1,0:T(8,128)(2,1)} %expansion_ref.1) | copy-start | bytes 9437188
  31.3 0.9 %copy-start.1 = (bf16[256,256]{1,0:T(8,128)(2,1)S(1)}, bf16[256,256]{1,0:T(8,128)(2,1)}, u32[]{:S(2)}) copy-start(bf16[256,256]{1,0:T(8,128)(2,1)} %shard_map.55.total_hbm) | copy-start | bytes 393220

commit v5 on v4

--- a/solution.py
+++ b/solution.py
@@ -78,8 +78,6 @@
     for start in range(0, rows, 128):
         row = order[:, start:start + 128]
         order_wide[start:start + 128, :] = jnp.broadcast_to(row, (128, 128)).T.astype(jnp.int16)
-    for load in loads[1:]:
-        load.wait()
 
     pl.semaphore_wait(barrier, levels + panels - 1)
     matrix_copy = pltpu.make_async_remote_copy(
@@ -92,6 +90,8 @@
     )
     matrix_copy.start()
 
+    for load in loads[1:]:
+        load.wait()
     source_tile = tile_of(rows, 512)
     for start in range(0, rows, source_tile):
         points[start:start + source_tile, :] = excitation[:, start:start + source_tile].T

time: 34.3 us -> 34.3 us (level)
  no operation moved by 1% of the time
where the time goes in v5:
time: 34.3 us; the launch traced here: 34.2 us
  Pallas kernels  33.2 us (97%)
  local copies, waits for them, and re-layouts  0.9 us (3%)
    pallas_call x1, Pallas kernels, per_device(): pl.pallas_call(functools.partial(coefficients_kernel, panels, levels), ou...  31.3 us
    pallas_call x1, Pallas kernels, per_device(): pl.pallas_call(expansion_kernel, out_shape=jax.ShapeDtypeStruct((2, exc,...  1.91 us
    unnamed x4, local copies, waits for them, and re-layouts  0.9 us

profile of v5, /device:TPU:0, one launch (start us, length us, event | category | flops | bytes accessed | tf_op | source)
XLA Modules:
  0.0 34.2 jit_solution(748836570573195262)
XLA Ops:
  0.0 0.0 copy-start
  0.0 31.3 %shard_map.55.total_hbm = bf16[256,256]{1,0:T(8,128)(2,1)} custom-call(bf16[2,128,3072]{2,1,0:T(8,128)(2,1)} %excitation_hbm.1, s32[1,3072]{1,0:T(1,128)} %order_hbm.1, bf16[2,256,3072]{2,1,0:T(8,128)(2,1)} %projection_hbm.1, bf16[3,2,256,512]{3,2,1,0:T(8,128)(2,1)} %transfer_hbm.1), custom_call_target="tpu_custom_call" | custom-call | tf_op jit(solution)/shard_map/pallas_call | solution.py:246
  31.3 0.0 copy-done
  31.3 0.0 copy-start.1
  31.3 0.9 %copy-done.1 = bf16[256,256]{1,0:T(8,128)(2,1)S(1)} copy-done((bf16[256,256]{1,0:T(8,128)(2,1)S(1)}, bf16[256,256]{1,0:T(8,128)(2,1)}, u32[]{:S(2)}) %copy-start.1) | copy-done | bytes 131096
  32.2 1.9 %shard_map.56 = bf16[2,128,3072]{2,1,0:T(8,128)(2,1)} custom-call(bf16[256,256]{1,0:T(8,128)(2,1)S(1)} %copy-done.1, bf16[2,256,3072]{2,1,0:T(8,128)(2,1)S(1)} %copy-done), custom_call_target="tpu_custom_call" | custom-call | tf_op jit(solution)/shard_map/pallas_call | solution.py:282
Async XLA Ops:
  0.0 31.3 %copy-start = (bf16[2,256,3072]{2,1,0:T(8,128)(2,1)S(1)}, bf16[2,256,3072]{2,1,0:T(8,128)(2,1)}, u32[]{:S(2)}) copy-start(bf16[2,256,3072]{2,1,0:T(8,128)(2,1)} %expansion_ref.1) | copy-start | bytes 9437188
  31.3 0.9 %copy-start.1 = (bf16[256,256]{1,0:T(8,128)(2,1)S(1)}, bf16[256,256]{1,0:T(8,128)(2,1)}, u32[]{:S(2)}) copy-start(bf16[256,256]{1,0:T(8,128)(2,1)} %shard_map.55.total_hbm) | copy-start | bytes 393220
